TPU v7x, 512 devices: a whole 4x4x16 slice. The times are simulated.
512 devices in a mesh: grp: 2 (over x_hi), seq: 32 (over x_lo, z), head: 8 (over y, core).
Axes of the slice: x: 4 (x_hi: 2, x_lo: 2; x = x_hi * 2 + x_lo), y: 4, z: 16, core: 2. Of those that a mesh axis runs over, the one named last changes fastest.
Arguments:
- features: bfloat16 [2, 32, 16, 32, 512], P('grp', 'seq', 'head'), may hold values from -6 to 6
- conv_weight: bfloat16 [3, 3, 3, 512, 16], replicated, may hold values from -0.0546875 to 0.0546875
- conv_bias: float32 [16], replicated, may hold values from -3 to 3
- token_order: int32 [4096], P('seq'), may hold values from 0 to 4095, each once
- embed_weight: bfloat16 [64, 3072], replicated, may hold values from -0.75 to 0.75
- norm_gain: float32 [3072], replicated, may hold values from 0.1 to 1.9
- qkv_weight: bfloat16 [3072, 3, 2048], P('seq', None, 'head'), may hold values from -0.109375 to 0.109375
- grad_out: bfloat16 [2, 4096, 2048], P('grp', 'seq', 'head'), may hold values from -6 to 6
Outputs:
- attended: bfloat16 [2, 4096, 2048], P('grp', 'seq', 'head')
- embed_grad: float32 [64, 3072], P(None, 'head')
All inputs are finite; a program needn't handle non-finite values.
Results may differ from a plain program's by a relative error of at most 0.0052.
Values may be sent and summed in bfloat16 or wider, within the bound.
No kernel may reach another device: no remote copies, remote signals or barrier semaphores. Data moves between devices by JAX's collectives and lax.ppermute only.
A program may use at most 64 MiB of HBM per device.

v0:
```python
import jax
import jax.numpy as jnp
from jax import lax
from jax.sharding import Mesh
from jax.sharding import PartitionSpec as P

D = 3072
HEAD_DIM = 64
SEQ = ("seq_0", "seq_1")
HEAD = ("head_0", "head_1")
GRP_SEQ = ("grp", "seq_0", "seq_1")


def shifted(value, axis, steps):
    count = lax.axis_size(axis)
    leading, last = (max(0, -steps), min(count, count - steps))
    return lax.ppermute(value, axis, [(source, source + steps) for source in range(leading, last)])


def extended(block, sides, width):
    for axis, dim in sides:
        count = lax.axis_size(axis)
        forward = [(i, i + 1) for i in range(count - 1)]
        backward = [(target, source) for source, target in forward]
        low = lax.ppermute(
            lax.slice_in_dim(block, block.shape[dim] - width, None, axis=dim), axis, forward
        )
        high = lax.ppermute(lax.slice_in_dim(block, 0, width, axis=dim), axis, backward)
        block = jnp.concatenate([low, block, high], axis=dim)
    return block


def from_everyone(array, axis):
    copies = jnp.broadcast_to(array, (lax.axis_size(axis), *array.shape))
    return lax.all_to_all(copies, axis, split_axis=0, concat_axis=0, tiled=True)


def joined_along(blocks, dim):
    lengths = list(blocks.shape[1:])
    lengths[dim] *= blocks.shape[0]
    return jnp.moveaxis(blocks, 0, dim).reshape(lengths)


def gather_axes(array, axes, dim):
    far, near = axes
    leading = from_everyone(array, far)
    blocks = jnp.swapaxes(from_everyone(leading, near), 0, 1)
    return joined_along(blocks.reshape(-1, *array.shape), dim)


def side_by_side(arrays, axis, dim, along):
    widths = [a.shape[along] for a in arrays]
    both = jnp.concatenate(arrays, axis=along)
    result = lax.all_gather(both, axis, axis=dim, tiled=True)
    return tuple(jnp.split(result, [sum(widths[:k]) for k in range(1, len(widths))], axis=along))


def split_up(array, dim, devices):
    before, after = (array.shape[:dim], array.shape[dim + 1 :])
    return jnp.moveaxis(array.reshape(*before, devices, -1, *after), dim, 0)


def sent_and_summed(array, axis, dim):
    devices = lax.axis_size(axis)
    blocks = lax.all_to_all(split_up(array, dim, devices), axis, 0, 0, tiled=True)
    return jnp.sum(blocks.astype(jnp.float32), axis=0)


def taken_together(array, axis):
    everything = from_everyone(array, axis)
    return jnp.sum(everything, axis=0)


def sent_and_summed_2(array, axis, dim):
    blocks = split_up(array, dim, lax.axis_size(axis))
    arrived = lax.all_to_all(blocks, axis, split_axis=0, concat_axis=0, tiled=True)
    return arrived.sum(axis=0)


def padded_to(lines, devices):
    spare = -lines.shape[0] % devices
    if not spare:
        return lines
    return jnp.concatenate([lines, jnp.zeros((spare, *lines.shape[1:]), lines.dtype)])


def gather_directly(array, axis, dim):
    return joined_along(from_everyone(array, axis), dim)


def nested_sum(array, axes):
    lines = array.reshape(-1, array.shape[-1])
    own = sent_and_summed_2(padded_to(lines, lax.axis_size(axes)), axes, 0)
    whole = gather_directly(own, axes, 0)
    return whole[: len(lines)].reshape(array.shape)


def patchify(latent):
    frames, rows, columns, channels = latent.shape
    blocks = latent.reshape(frames, rows // 2, 2, columns // 2, 2, channels)
    blocks = jnp.transpose(blocks, (0, 1, 3, 2, 4, 5))
    return blocks.reshape(frames * (rows // 2) * (columns // 2), 4 * channels)


def encode_tile(tile, conv_weight, conv_bias):
    frames, rows, columns, channels = tile.shape
    hops = (frames + 1) // frames
    earlier = []
    for hop in range(hops, 0, -1):
        earlier.append(shifted(tile, SEQ, hop))
    stacked = jnp.concatenate(earlier + [tile], axis=0)
    padded = extended(stacked, ((HEAD, 1),), 1)
    padded = jnp.pad(padded, ((0, 0), (0, 0), (1, 1), (0, 0)))
    total = jnp.zeros((frames * rows * columns, conv_weight.shape[-1]), jnp.float32) + conv_bias
    for a in range(3):
        for b in range(3):
            for e in range(3):
                piece = padded[a : a + frames, b : b + rows, e : e + columns].reshape(-1, channels)
                total = total + jnp.dot(
                    piece, conv_weight[a, b, e], preferred_element_type=jnp.float32
                )
    return total.astype(jnp.bfloat16).reshape(frames, rows, columns, conv_weight.shape[-1])


def head_major(matrix, head_local):
    count = matrix.shape[0]
    return jnp.transpose(matrix.reshape(count, head_local, HEAD_DIM), (1, 0, 2))


def row_major(stacked):
    heads_here, count, size = stacked.shape
    return jnp.transpose(stacked, (1, 0, 2)).reshape(count, heads_here * size)


def head_forward(operands):
    query, keys, values, cotan = operands
    factor = HEAD_DIM ** (-0.5)
    scores = jnp.dot(query, keys.T, preferred_element_type=jnp.float32) * factor
    top = jnp.max(scores, axis=-1, keepdims=True)
    lse = top + jnp.log(jnp.sum(jnp.exp(scores - top), axis=-1, keepdims=True))
    probs = jnp.exp(scores - lse)
    probs_low = probs.astype(jnp.bfloat16)
    output = jnp.dot(probs_low, values, preferred_element_type=jnp.float32).astype(jnp.bfloat16)
    delta = jnp.sum(cotan.astype(jnp.float32) * output.astype(jnp.float32), axis=-1, keepdims=True)
    dprob = jnp.dot(cotan, values.T, preferred_element_type=jnp.float32)
    dscore = (probs * (dprob - delta)).astype(jnp.bfloat16)
    grad_q = jnp.dot(dscore, keys, preferred_element_type=jnp.float32) * factor
    return (output, lse[:, 0], delta[:, 0], grad_q)


def head_backward(operands):
    query, cotan, lse_piece, delta_piece, own_keys, own_values = operands
    factor = HEAD_DIM ** (-0.5)
    scores = jnp.dot(query, own_keys.T, preferred_element_type=jnp.float32) * factor
    probs = jnp.exp(scores - lse_piece[:, None])
    value_add = jnp.dot(probs.astype(jnp.bfloat16).T, cotan, preferred_element_type=jnp.float32)
    dprob = jnp.dot(cotan, own_values.T, preferred_element_type=jnp.float32)
    dscore = (probs * (dprob - delta_piece[:, None])).astype(jnp.bfloat16)
    key_add = jnp.dot(dscore.T, query, preferred_element_type=jnp.float32)
    return (key_add, value_add)


def per_device(
    features, conv_weight, conv_bias, token_order, embed_weight, norm_gain, qkv_weight, grad_out
):
    tile = encode_tile(features[0], conv_weight, conv_bias)
    frames, rows, columns, channels = tile.shape
    every = gather_axes(tile[None], (("seq_0", "seq_1"), ("head_0", "head_1")), 0)
    seq_count = lax.axis_size(SEQ)
    head_count = lax.axis_size(HEAD)
    every = every.reshape(seq_count, head_count, frames, rows, columns, channels)
    every = jnp.transpose(every, (0, 2, 1, 3, 4, 5))
    whole = every.reshape(seq_count * frames, head_count * rows, columns, channels)
    patches = patchify(whole)
    tokens = jnp.take(patches, token_order, axis=0)
    local_rows = tokens.shape[0]
    mixed = jnp.dot(tokens, embed_weight, preferred_element_type=jnp.float32)
    inverse = lax.rsqrt(jnp.mean(mixed * mixed, axis=-1, keepdims=True) + 1e-06)
    normal = mixed * inverse
    hidden = (normal * norm_gain).astype(jnp.bfloat16)
    full_weight = lax.all_gather(qkv_weight, SEQ, axis=0, tiled=True)
    local_width = full_weight.shape[2]
    head_local = local_width // HEAD_DIM
    flat_weight = full_weight.reshape(D, 3 * local_width)
    proj = jnp.dot(hidden, flat_weight, preferred_element_type=jnp.float32).astype(jnp.bfloat16)
    proj = proj.reshape(local_rows, 3, local_width)
    query = proj[:, 0]
    keys_all, values_all = side_by_side((proj[:, 1], proj[:, 2]), SEQ, 0, 1)
    cotan = grad_out[0]
    output_h, lse_h, delta_h, grad_q_h = lax.map(
        head_forward,
        (
            head_major(query, head_local),
            head_major(keys_all, head_local),
            head_major(values_all, head_local),
            head_major(cotan, head_local),
        ),
    )
    output = row_major(output_h)
    grad_q = row_major(grad_q_h)
    lse_all, delta_all = side_by_side((jnp.transpose(lse_h), jnp.transpose(delta_h)), SEQ, 0, 1)
    own_keys = head_major(proj[:, 1], head_local)
    own_values = head_major(proj[:, 2], head_local)
    query_piece, cotan_piece = side_by_side((query, cotan), SEQ, 0, 1)
    lse_piece = jnp.transpose(lse_all)
    delta_piece = jnp.transpose(delta_all)
    key_add, value_add = lax.map(
        head_backward,
        (
            head_major(query_piece, head_local),
            head_major(cotan_piece, head_local),
            lse_piece,
            delta_piece,
            own_keys,
            own_values,
        ),
    )
    grad_k = row_major(key_add * HEAD_DIM ** (-0.5))
    grad_v = row_major(value_add)
    grads = (
        jnp.stack([grad_q, grad_k, grad_v], axis=1)
        .reshape(local_rows, 3 * local_width)
        .astype(jnp.bfloat16)
    )
    back_part = lax.dot_general(
        grads, flat_weight, (((1,), (1,)), ((), ())), preferred_element_type=jnp.float32
    )
    head_count_d = lax.axis_size(HEAD)
    width_dev = D // head_count_d
    start_col = lax.axis_index(HEAD) * width_dev
    normal_own = lax.dynamic_slice_in_dim(normal, start_col, width_dev, 1)
    gain_own = lax.dynamic_slice_in_dim(norm_gain, start_col, width_dev, 0)
    back_own = sent_and_summed(back_part.astype(jnp.bfloat16), HEAD, 1)
    scaled_own = back_own * gain_own
    inner_part = jnp.sum(scaled_own * normal_own, axis=-1, keepdims=True)
    inner = taken_together(inner_part, HEAD) / D
    dmixed_own = inverse * (scaled_own - normal_own * inner)
    embed_part = jnp.dot(
        tokens.astype(jnp.float32).T,
        dmixed_own,
        preferred_element_type=jnp.float32,
        precision=lax.Precision.HIGHEST,
    )
    embed_grad = nested_sum(embed_part, GRP_SEQ)
    attended = output.reshape(1, local_rows, local_width)
    return (attended, embed_grad)


def solution(mesh):
    torus = Mesh(
        mesh.devices.reshape(mesh.shape["grp"], 2, 16, 4, 2),
        ("grp", "seq_0", "seq_1", "head_0", "head_1"),
    )
    return jax.shard_map(
        per_device,
        mesh=torus,
        in_specs=(
            P("grp", SEQ, HEAD, None, None),
            P(),
            P(),
            P(SEQ),
            P(),
            P(),
            P(SEQ, None, HEAD),
            P("grp", SEQ, HEAD),
        ),
        out_specs=(P("grp", SEQ, HEAD), P(None, HEAD)),
        check_vma=False,
    )
```

profile of v0, /device:TPU:2, one launch (start us, length us, event | category | flops | bytes accessed | tf_op | source)
XLA Modules:
  0.0 568.6 jit_solution(3382214532136301586)
XLA Ops:
  7.2 5.3 collective-permute-start
  16.4 5.2 collective-permute-done
  36.5 23.9 %all_to_all.33 = bf16[32,2,512]{2,1,0:T(2,128)(2,1)S(1)} all-to-all(bf16[32,2,512]{2,1,0:T(2,128)(2,1)S(1)} %reshape.224), channel_id=1, replica_groups=mesh['grp'=2,'seq_0'=2,'seq_1'=16,'head_0'=4,'head_1'=2] {'seq_0','seq_1'}, dimensions={0} | all-to-all | bytes 131072 | tf_op jit(solution)/shard_map/all_to_all | solution.py:35
  64.2 7.5 %all-to-all-start.1 = ((bf16[8,2,16384]{2,1,0:T(2,128)(2,1)}), bf16[8,2,16384]{2,1,0:T(2,128)(2,1)S(1)}, u32[]{:S(2)}, u32[]{:S(2)}) async-start(bf16[8,2,16384]{2,1,0:T(2,128)(2,1)} %reshape.226), calls=%async_computation.1 | async-start | bytes 1048576 | tf_op jit(solution)/shard_map/all_to_all | solution.py:35
  71.7 10.3 %all-to-all-done.1 = bf16[8,2,16384]{2,1,0:T(2,128)(2,1)S(1)} async-done(((bf16[8,2,16384]{2,1,0:T(2,128)(2,1)}), bf16[8,2,16384]{2,1,0:T(2,128)(2,1)S(1)}, u32[]{:S(2)}, u32[]{:S(2)}) %all-to-all-start.1) | async-done | bytes 524320 | tf_op jit(solution)/shard_map/all_to_all | solution.py:35
  83.0 9.7 %copy.86 = bf16[32,8,16,2,2,16]{5,4,3,2,1,0:T(2,128)(2,1)} copy(bf16[32,8,16,2,2,16]{0,5,4,2,3,1:T(8,128)(2,1)S(1)} %bitcast.364) | data formatting | bytes 1048576 | tf_op jit(solution)/shard_map/reshape | solution.py:102
  92.7 8.0 %reshape.223 = bf16[4096,64]{1,0:T(8,128)(2,1)S(1)} reshape(bf16[32,8,16,2,2,16]{5,4,3,2,1,0:T(2,128)(2,1)} %copy.86) | data formatting | bytes 1048576 | tf_op jit(solution)/shard_map/reshape | solution.py:102
  102.1 64.1 %all-gather.4.cloned.1.call-done = bf16[3072,3,256]{2,0,1:T(8,128)(2,1)} async-done(((bf16[96,3,256]{2,0,1:T(8,128)(2,1)}), bf16[3072,3,256]{2,0,1:T(8,128)(2,1)}) %all-gather.4.cloned.1.call-update) | async-done | bytes 4718608 | tf_op jit(solution)/shard_map/all_gather | solution.py:181
  166.2 6.7 %copy.67 = bf16[3072,3,256]{0,2,1:T(8,128)(2,1)} copy(bf16[3072,3,256]{2,0,1:T(8,128)(2,1)} %all-gather.4.cloned.1.call-done) | data formatting | bytes 9437184 | tf_op jit(solution)/shard_map/all_gather | solution.py:181
  172.9 4.0 convolution_convert_fusion.1
  179.0 135.7 %all-gather.6.cloned.1.call-done = bf16[4096,512]{0,1:T(8,128)(2,1)} async-done(((bf16[128,512]{0,1:T(8,128)(2,1)}), bf16[4096,512]{0,1:T(8,128)(2,1)}) %all-gather.6.cloned.1.call-update) | async-done | bytes 4194320 | tf_op jit(solution)/shard_map/all_gather | solution.py:54
  314.7 4.6 fusion.160
  319.4 23.7 %while.30 = (s32[]{:T(128)}, bf16[4,128,64]{1,2,0:T(8,128)(2,1)S(1)}, f32[4,128]{1,0:T(4,128)S(1)}, f32[4,128]{1,0:T(4,128)S(1)}, bf16[4,128,64]{1,2,0:T(8,128)(...) while((s32[]{:T(128)}, ...), condition=%wide.region_5.6_spmd.clone, body=%wide.region_1.0_spmd.sunk.clone | while | flops 273727232 | bytes 10628201 | solution.py:190
  343.1 61.5 %all_gather.15 = f32[4096,8]{0,1:T(8,128)S(1)} all-gather(f32[128,8]{0,1:T(8,128)S(1)} %pad_maximum_fusion.13), channel_id=1, replica_groups=mesh['grp'=2,'seq_0'=2,'seq_1'=16,'head_0'=4,'head_1'=2] {'seq_0','seq_1'}, dimensions={0}, use_global_device_ids=true | all-gather | bytes 135168 | tf_op jit(solution)/shard_map/all_gather | solution.py:54
  404.6 50.6 %all-gather.8.cloned.1.call-done = bf16[4096,512]{0,1:T(8,128)(2,1)} async-done(((bf16[128,512]{0,1:T(8,128)(2,1)}), bf16[4096,512]{0,1:T(8,128)(2,1)}) %all-gather.8.cloned.1.call-update) | async-done | bytes 4194320 | tf_op jit(solution)/shard_map/all_gather | solution.py:54
  455.3 4.8 fusion.159
  460.0 22.7 %while.31 = (s32[]{:T(128)}, f32[4,128,64]{1,2,0:T(8,128)S(1)}, bf16[4,128,64]{1,2,0:T(8,128)(2,1)S(1)}, bf16[4,4096,64]{1,2,0:T(8,128)(2,1)}, bf16[4,128,64]{1,...) while((s32[]{:T(128)}, f32[4,128,64]{1,2,0:T(8,128)S(1)}, ...), condition=%wide.region_7.8_spmd.clone, body=%wide.region_6.7_spmd.sunk.clone | while | flops 271581184 | bytes 8589409 | solution.py:207
  483.1 4.0 fusion.61
  488.0 4.1 all-to-all-start.2
  492.2 13.1 %all-to-all-done.2 = bf16[8,128,384]{2,1,0:T(8,128)(2,1)S(1)} async-done(((bf16[8,128,384]{2,1,0:T(8,128)(2,1)}), bf16[8,128,384]{2,1,0:T(8,128)(2,1)S(1)}, u32[]{:S(2)}, u32[]{:S(2)}) %all-to-all-start.2) | async-done | bytes 786464 | tf_op jit(solution)/shard_map/all_to_all | solution.py:65
  506.5 7.6 %all_to_all.34 = f32[8,128,1]{1,2,0:T(1,128)S(1)} all-to-all(f32[8,128,1]{1,2,0:T(1,128)S(1)} %broadcast_in_dim.62), channel_id=1, replica_groups=mesh['grp'=2,'seq_0'=2,'seq_1'=16,'head_0'=4,'head_1'=2] {'head_0','head..., dimensions={0} | all-to-all | bytes 8192 | tf_op jit(solution)/shard_map/all_to_all | solution.py:35
  515.5 24.9 %all_to_all.35 = f32[64,1,384]{2,1,0:T(1,128)S(1)} all-to-all(f32[64,1,384]{2,1,0:T(1,128)S(1)} %copy.84), channel_id=1, replica_groups=mesh['grp'=2,'seq_0'=2,'seq_1'=16,'head_0'=4,'head_1'=2] {'grp','seq_0',..., dimensions={0} | all-to-all | bytes 196608 | tf_op jit(solution)/shard_map/all_to_all | solution.py:76
  541.2 6.0 %all-to-all-start.5 = ((f32[64,1,384]{2,1,0:T(1,128)}), f32[64,1,384]{2,1,0:T(1,128)S(1)}, u32[]{:S(2)}, u32[]{:S(2)}) async-start(f32[64,1,384]{2,1,0:T(1,128)} %broadcast_in_dim.63), calls=%async_computation.5 | async-start | bytes 196608 | tf_op jit(solution)/shard_map/all_to_all | solution.py:35
  547.9 13.5 %all-to-all-done.5 = f32[64,1,384]{2,1,0:T(1,128)S(1)} async-done(((f32[64,1,384]{2,1,0:T(1,128)}), f32[64,1,384]{2,1,0:T(1,128)S(1)}, u32[]{:S(2)}, u32[]{:S(2)}) %all-to-all-start.5) | async-done | bytes 98336 | tf_op jit(solution)/shard_map/all_to_all | solution.py:35
  (156 shorter events, 79.1 us)
Async XLA Ops:
  7.2 94.2 %copy-start = (bf16[64,3072]{1,0:T(8,128)(2,1)S(1)}, bf16[64,3072]{1,0:T(8,128)(2,1)}, u32[]{:S(2)}) copy-start(bf16[64,3072]{1,0:T(8,128)(2,1)} %param.16) | copy-start | bytes 1179652
  7.2 25.0 %copy-start.2 = (bf16[1,1,2,32,512]{4,3,2,1,0:T(8,128)(2,1)S(1)}, bf16[1,1,2,32,512]{4,3,2,1,0:T(8,128)(2,1)}, u32[]{:S(2)}) copy-start(bf16[1,1,2,32,512]{4,3,2,1,0:T(8,128)(2,1)} %param.12) | copy-start | bytes 196612
  7.2 159.0 %all-gather.4.cloned.1.call-start = ((), (), s32[]{:S(2)}) async-start(), calls=%async_computation.6 | async-start | bytes 4866048 | tf_op jit(solution)/shard_map/all_gather | solution.py:181
  7.2 14.4 %collective-permute-start = (bf16[1,2,32,512]{3,2,1,0:T(8,128)(2,1)}, bf16[1,2,32,512]{3,2,1,0:T(8,128)(2,1)S(1)}, u32[]{:S(2)}, u32[]{:S(2)}) collective-permute-start(bf16[1,2,32,512]{3,2,1,0:T(8,128)(2,1)} %bitcast.368), channel_id=1, source_target_pairs={{0,16},{8,24},{16,32},{24,40},{32,48},{40,56},{48,64},{56,72},{64,... | collective-permute-start | bytes 196616 | tf_op jit(solution)/shard_map/ppermute | solution.py:17
  12.6 11.3 %collective-permute-start.1 = (bf16[1,2,32,512]{3,2,1,0:T(8,128)(2,1)}, bf16[1,2,32,512]{3,2,1,0:T(8,128)(2,1)S(1)}, u32[]{:S(2)}, u32[]{:S(2)}) collective-permute-start(bf16[1,2,32,512]{3,2,1,0:T(8,128)(2,1)} %bitcast.369), channel_id=1, source_target_pairs={{0,8},{8,16},{16,24},{24,32},{32,40},{40,48},{48,56},{56,64},{64,7... | collective-permute-start | bytes 196616 | tf_op jit(solution)/shard_map/ppermute | solution.py:17
  24.7 3.0 collective-permute-start.2
  26.3 6.2 %copy-start.3 = (bf16[3,3,3,512,16]{3,4,2,1,0:T(8,128)(2,1)S(1)}, bf16[3,3,3,512,16]{3,4,2,1,0:T(8,128)(2,1)}, u32[]{:S(2)}) copy-start(bf16[3,3,3,512,16]{3,4,2,1,0:T(8,128)(2,1)} %param.13) | copy-start | bytes 1327108
  26.3 4.9 collective-permute-start.3
  28.5 5.0 copy-start.6
  61.5 10.2 %copy-start.7 = (s32[128]{0:T(128)S(1)}, s32[128]{0:T(128)}, u32[]{:S(2)}) copy-start(s32[128]{0:T(128)} %param.15) | copy-start | bytes 1540
  64.2 17.8 %all-to-all-start.1 = ((bf16[8,2,16384]{2,1,0:T(2,128)(2,1)}), bf16[8,2,16384]{2,1,0:T(2,128)(2,1)S(1)}, u32[]{:S(2)}, u32[]{:S(2)}) async-start(bf16[8,2,16384]{2,1,0:T(2,128)(2,1)} %reshape.226), calls=%async_computation.1 | async-start | bytes 1048576 | tf_op jit(solution)/shard_map/all_to_all | solution.py:35
  71.6 243.1 %all-gather.6.cloned.1.call-start = ((), (), s32[]{:S(2)}) async-start(), calls=%async_computation.7 | async-start | bytes 4325376 | tf_op jit(solution)/shard_map/all_gather | solution.py:54
  102.1 70.9 %copy-start.1 = (f32[128,3072]{1,0:T(8,128)}, f32[128,3072]{1,0:T(8,128)S(1)}, u32[]{:S(2)}) copy-start(f32[128,3072]{1,0:T(8,128)S(1)} %broadcast_multiply_fusion) | copy-start | bytes 4718596
  102.1 70.9 %copy-start.5 = (f32[3072]{0:T(1024)S(1)}, f32[3072]{0:T(1024)}, u32[]{:S(2)}) copy-start(f32[3072]{0:T(1024)} %param.17) | copy-start | bytes 36868
  172.9 5.2 copy-start.4
  177.9 277.4 %all-gather.8.cloned.1.call-start = ((), (), s32[]{:S(2)}) async-start(), calls=%async_computation.8 | async-start | bytes 4325376 | tf_op jit(solution)/shard_map/all_gather | solution.py:54
  488.0 17.3 %all-to-all-start.2 = ((bf16[8,128,384]{2,1,0:T(8,128)(2,1)}), bf16[8,128,384]{2,1,0:T(8,128)(2,1)S(1)}, u32[]{:S(2)}, u32[]{:S(2)}) async-start(bf16[8,128,384]{2,1,0:T(8,128)(2,1)} %bitcast.294), calls=%async_computation.2 | async-start | bytes 1572864 | tf_op jit(solution)/shard_map/all_to_all | solution.py:65
  541.2 20.2 %all-to-all-start.5 = ((f32[64,1,384]{2,1,0:T(1,128)}), f32[64,1,384]{2,1,0:T(1,128)S(1)}, u32[]{:S(2)}, u32[]{:S(2)}) async-start(f32[64,1,384]{2,1,0:T(1,128)} %broadcast_in_dim.63), calls=%async_computation.5 | async-start | bytes 196608 | tf_op jit(solution)/shard_map/all_to_all | solution.py:35
Sparse Core Ops, SparseCore 0:
  26.4 139.7 all-gather.3
  178.0 136.6 all-gather.5
  316.7 138.4 all-gather.7
where the time goes:
time: 570 us; the launch traced here: 569 us
  waiting for transfers between devices  297 us (52%)
  blocking collectives  118 us (21%)
  matrix products  57.1 us (10%)
  local copies, waits for them, and re-layouts  44.1 us (8%)
  starting transfers between devices  30 us (5%)
  between operations  14.2 us (2%)
  other arithmetic  7.52 us (1%)
    all_gather x2, waiting for transfers between devices, side_by_side(): result = lax.all_gather(both, axis, axis=dim, tiled=True)  186 us
    all_gather x1, waiting for transfers between devices, per_device(): full_weight = lax.all_gather(qkv_weight, SEQ, axis=0, tiled=True)  64.1 us
    all_gather x1, blocking collectives, side_by_side(): result = lax.all_gather(both, axis, axis=dim, tiled=True)  61.5 us
    all_to_all x2, blocking collectives, from_everyone(): return lax.all_to_all(copies, axis, split_axis=0, concat_axis=0, tiled=True)  31.6 us
    all_to_all x1, blocking collectives, sent_and_summed_2(): lax.all_to_all(blocks, axis, split_axis=0, concat_axis=0, tiled=True)  24.9 us
    all_to_all x2, waiting for transfers between devices, from_everyone(): return lax.all_to_all(copies, axis, split_axis=0, concat_axis=0, tiled=True)  23.7 us
    reshape x2, local copies, waits for them, and re-layouts, patchify(): return blocks.reshape(frames * (rows // 2) * (columns // 2), 4 * channels)  17.6 us
    all_to_all x2, starting transfers between devices, from_everyone(): return lax.all_to_all(copies, axis, split_axis=0, concat_axis=0, tiled=True)  13.5 us
  transfers between devices with their start and end apart: 10, of which 9 were waited for; matrix products, arithmetic and copies ran while one was open for 10% of the time, Pallas kernels for 0%

commit v1 on v0

--- a/solution.py
+++ b/solution.py
@@ -178,7 +178,9 @@
     inverse = lax.rsqrt(jnp.mean(mixed * mixed, axis=-1, keepdims=True) + 1e-06)
     normal = mixed * inverse
     hidden = (normal * norm_gain).astype(jnp.bfloat16)
-    full_weight = lax.all_gather(qkv_weight, SEQ, axis=0, tiled=True)
+    full_weight = jnp.concatenate(
+        lax.all_to_all(jnp.stack([qkv_weight] * lax.axis_size(SEQ)), SEQ, 0, 0), axis=0
+    )
     local_width = full_weight.shape[2]
     head_local = local_width // HEAD_DIM
     flat_weight = full_weight.reshape(D, 3 * local_width)

time: 570 us -> 717 us (1.26)
  waiting for transfers between devices: 297 us -> 412 us
  blocking collectives: 118 us -> 136 us
  local copies, waits for them, and re-layouts: 44.1 us -> 60.6 us
    all_to_all x0 -> x1, waiting for transfers between devices: none -> 185 us  [per_device(): lax.all_to_all(jnp.stack([qkv_weight] * lax.axis_size(SEQ)), SEQ, 0, 0)]
    all_gather x1 -> x0, waiting for transfers between devices: 64.1 us -> none  [per_device(): full_weight = lax.all_gather(qkv_weight, SEQ, axis=0, tiled=True)]
    all_to_all x2 -> x3, blocking collectives: 31.6 us -> 48.6 us  [from_everyone(): return lax.all_to_all(copies, axis, split_axis=0, concat_axis=0, tiled=True)]
    another operation x3 -> x2, local copies, waits for them, and re-layouts: 0.32 us -> 15.7 us  [the longest x1 12.1 us: per_device(): flat_weight = full_weight.reshape(D, 3 * local_width)]
    all_to_all x2 -> x1, waiting for transfers between devices: 23.7 us -> 13.5 us  [from_everyone(): return lax.all_to_all(copies, axis, split_axis=0, concat_axis=0, tiled=True)]
    all_to_all x0 -> x1, local copies, waits for them, and re-layouts: none -> 8.37 us  [per_device(): lax.all_to_all(jnp.stack([qkv_weight] * lax.axis_size(SEQ)), SEQ, 0, 0)]
    all_to_all x2 -> x1, starting transfers between devices: 13.5 us -> 6.01 us  [from_everyone(): return lax.all_to_all(copies, axis, split_axis=0, concat_axis=0, tiled=True)]
  transfers between devices with their start and end apart: 10 -> 9, of which waited for: 9 -> 8; matrix products, arithmetic and copies ran while one was open for 10% -> 7% of each run, Pallas kernels for 0% -> 0%
where the time goes in v1:
time: 717 us; the launch traced here: 715 us
  waiting for transfers between devices  412 us (57%)
  blocking collectives  136 us (19%)
  local copies, waits for them, and re-layouts  60.6 us (8%)
  matrix products  56.3 us (8%)
  starting transfers between devices  29.4 us (4%)
  between operations  14.5 us (2%)
    all_gather x2, waiting for transfers between devices, side_by_side(): result = lax.all_gather(both, axis, axis=dim, tiled=True)  189 us
    all_to_all x1, waiting for transfers between devices, per_device(): lax.all_to_all(jnp.stack([qkv_weight] * lax.axis_size(SEQ)), SEQ, 0, 0)  185 us
    all_gather x1, blocking collectives, side_by_side(): result = lax.all_gather(both, axis, axis=dim, tiled=True)  61.7 us
    all_to_all x3, blocking collectives, from_everyone(): return lax.all_to_all(copies, axis, split_axis=0, concat_axis=0, tiled=True)  48.6 us
    all_to_all x1, blocking collectives, sent_and_summed_2(): lax.all_to_all(blocks, axis, split_axis=0, concat_axis=0, tiled=True)  25.2 us
    reshape x2, local copies, waits for them, and re-layouts, patchify(): return blocks.reshape(frames * (rows // 2) * (columns // 2), 4 * channels)  17.6 us
  transfers between devices with their start and end apart: 9, of which 8 were waited for; matrix products, arithmetic and copies ran while one was open for 7% of the time, Pallas kernels for 0%

profile of v1, /device:TPU:2, one launch (start us, length us, event | category | flops | bytes accessed | tf_op | source)
XLA Modules:
  0.0 715.0 jit_solution(4141928763236695548)
XLA Ops:
  7.2 5.3 collective-permute-start
  16.3 5.2 collective-permute-done
  36.4 24.1 %all_to_all.38 = bf16[32,2,512]{2,1,0:T(2,128)(2,1)S(1)} all-to-all(bf16[32,2,512]{2,1,0:T(2,128)(2,1)S(1)} %reshape.227), channel_id=1, replica_groups=mesh['grp'=2,'seq_0'=2,'seq_1'=16,'head_0'=4,'head_1'=2] {'seq_0','seq_1'}, dimensions={0} | all-to-all | bytes 131072 | tf_op jit(solution)/shard_map/all_to_all | solution.py:35
  63.5 16.9 %all_to_all.39 = bf16[8,2,16384]{2,1,0:T(2,128)(2,1)S(1)} all-to-all(bf16[8,2,16384]{2,1,0:T(2,128)(2,1)S(1)} %reshape.229), channel_id=1, replica_groups=mesh['grp'=2,'seq_0'=2,'seq_1'=16,'head_0'=4,'head_1'=2] {'head_0','head..., dimensions={0} | all-to-all | bytes 1048576 | tf_op jit(solution)/shard_map/all_to_all | solution.py:35
  84.1 6.3 all-to-all-start.2
  91.7 9.6 %copy.75 = bf16[32,8,16,2,2,16]{5,4,3,2,1,0:T(2,128)(2,1)} copy(bf16[32,8,16,2,2,16]{0,5,4,2,3,1:T(8,128)(2,1)S(1)} %bitcast.364) | data formatting | bytes 1048576 | tf_op jit(solution)/shard_map/reshape | solution.py:102
  101.4 8.0 %reshape.226 = bf16[4096,64]{1,0:T(8,128)(2,1)S(1)} reshape(bf16[32,8,16,2,2,16]{5,4,3,2,1,0:T(2,128)(2,1)} %copy.75) | data formatting | bytes 1048576 | tf_op jit(solution)/shard_map/reshape | solution.py:102
  110.8 185.3 %all-to-all-done.2 = bf16[32,96,3,256]{3,1,2,0:T(8,128)(2,1)} async-done(((bf16[32,96,3,256]{3,1,2,0:T(8,128)(2,1)}), bf16[32,96,3,256]{3,1,2,0:T(8,128)(2,1)}, u32[]{:S(2)}, u32[]{:S(2)}) %all-to-all-start.2) | async-done | bytes 4718624 | tf_op jit(solution)/shard_map/all_to_all | solution.py:182
  296.1 8.4 %copy.59 = bf16[32,96,3,256]{1,0,3,2:T(8,128)(2,1)} copy(bf16[32,96,3,256]{3,1,2,0:T(8,128)(2,1)} %all-to-all-done.2) | data formatting | bytes 9437184 | tf_op jit(solution)/shard_map/all_to_all | solution.py:182
  304.4 12.1 %reshape_reshape.6 = bf16[3072,768]{0,1:T(8,128)(2,1)} reshape(bf16[32,96,3,256]{1,0,3,2:T(8,128)(2,1)} %copy.59) | data formatting | bytes 9437184 | tf_op jit(solution)/shard_map/reshape;reshape | solution.py:186
  316.6 4.0 convolution_convert_fusion.2
  322.4 138.6 %all-gather.3.cloned.1.call-done = bf16[4096,512]{0,1:T(8,128)(2,1)} async-done(((bf16[128,512]{0,1:T(8,128)(2,1)}), bf16[4096,512]{0,1:T(8,128)(2,1)}) %all-gather.3.cloned.1.call-update) | async-done | bytes 4194320 | tf_op jit(solution)/shard_map/all_gather | solution.py:54
  461.0 4.7 fusion.153
  465.7 23.7 %while.30 = (s32[]{:T(128)}, bf16[4,128,64]{1,2,0:T(8,128)(2,1)S(1)}, f32[4,128]{1,0:T(4,128)S(1)}, f32[4,128]{1,0:T(4,128)S(1)}, bf16[4,128,64]{1,2,0:T(8,128)(...) while((s32[]{:T(128)}, ...), condition=%wide.region_5.6_spmd.clone, body=%wide.region_1.0_spmd.sunk.clone | while | flops 273727232 | bytes 10628201 | solution.py:192
  489.4 61.7 %all_gather.11 = f32[4096,8]{0,1:T(8,128)S(1)} all-gather(f32[128,8]{0,1:T(8,128)S(1)} %pad_maximum_fusion.14), channel_id=1, replica_groups=mesh['grp'=2,'seq_0'=2,'seq_1'=16,'head_0'=4,'head_1'=2] {'seq_0','seq_1'}, dimensions={0}, use_global_device_ids=true | all-gather | bytes 135168 | tf_op jit(solution)/shard_map/all_gather | solution.py:54
  551.2 50.3 %all-gather.5.cloned.1.call-done = bf16[4096,512]{0,1:T(8,128)(2,1)} async-done(((bf16[128,512]{0,1:T(8,128)(2,1)}), bf16[4096,512]{0,1:T(8,128)(2,1)}) %all-gather.5.cloned.1.call-update) | async-done | bytes 4194320 | tf_op jit(solution)/shard_map/all_gather | solution.py:54
  601.5 4.8 fusion.152
  606.2 22.7 %while.31 = (s32[]{:T(128)}, f32[4,128,64]{1,2,0:T(8,128)S(1)}, bf16[4,128,64]{1,2,0:T(8,128)(2,1)S(1)}, bf16[4,4096,64]{1,2,0:T(8,128)(2,1)}, bf16[4,128,64]{1,...) while((s32[]{:T(128)}, f32[4,128,64]{1,2,0:T(8,128)S(1)}, ...), condition=%wide.region_7.8_spmd.clone, body=%wide.region_6.7_spmd.sunk.clone | while | flops 271581184 | bytes 8589409 | solution.py:209
  633.1 4.8 all-to-all-start.3
  638.0 13.1 %all-to-all-done.3 = bf16[8,128,384]{2,1,0:T(8,128)(2,1)S(1)} async-done(((bf16[8,128,384]{2,1,0:T(8,128)(2,1)}), bf16[8,128,384]{2,1,0:T(8,128)(2,1)S(1)}, u32[]{:S(2)}, u32[]{:S(2)}) %all-to-all-start.3) | async-done | bytes 786464 | tf_op jit(solution)/shard_map/all_to_all | solution.py:65
  652.2 7.6 %all_to_all.40 = f32[8,128,1]{1,2,0:T(1,128)S(1)} all-to-all(f32[8,128,1]{1,2,0:T(1,128)S(1)} %broadcast_in_dim.62), channel_id=1, replica_groups=mesh['grp'=2,'seq_0'=2,'seq_1'=16,'head_0'=4,'head_1'=2] {'head_0','head..., dimensions={0} | all-to-all | bytes 8192 | tf_op jit(solution)/shard_map/all_to_all | solution.py:35
  661.2 25.2 %all_to_all.41 = f32[64,1,384]{2,1,0:T(1,128)S(1)} all-to-all(f32[64,1,384]{2,1,0:T(1,128)S(1)} %copy.73), channel_id=1, replica_groups=mesh['grp'=2,'seq_0'=2,'seq_1'=16,'head_0'=4,'head_1'=2] {'grp','seq_0',..., dimensions={0} | all-to-all | bytes 196608 | tf_op jit(solution)/shard_map/all_to_all | solution.py:76
  687.3 6.0 all-to-all-start.6
  694.0 13.5 %all-to-all-done.6 = f32[64,1,384]{2,1,0:T(1,128)S(1)} async-done(((f32[64,1,384]{2,1,0:T(1,128)}), f32[64,1,384]{2,1,0:T(1,128)S(1)}, u32[]{:S(2)}, u32[]{:S(2)}) %all-to-all-start.6) | async-done | bytes 98336 | tf_op jit(solution)/shard_map/all_to_all | solution.py:35
  (154 shorter events, 84.8 us)
Async XLA Ops:
  7.2 102.9 %copy-start = (bf16[64,3072]{1,0:T(8,128)(2,1)S(1)}, bf16[64,3072]{1,0:T(8,128)(2,1)}, u32[]{:S(2)}) copy-start(bf16[64,3072]{1,0:T(8,128)(2,1)} %param.16) | copy-start | bytes 1179652
  7.2 25.1 %copy-start.3 = (bf16[3,3,3,512,16]{3,4,2,1,0:T(8,128)(2,1)S(1)}, bf16[3,3,3,512,16]{3,4,2,1,0:T(8,128)(2,1)}, u32[]{:S(2)}) copy-start(bf16[3,3,3,512,16]{3,4,2,1,0:T(8,128)(2,1)} %param.13) | copy-start | bytes 1327108
  7.2 14.4 %collective-permute-start = (bf16[1,2,32,512]{3,2,1,0:T(8,128)(2,1)}, bf16[1,2,32,512]{3,2,1,0:T(8,128)(2,1)S(1)}, u32[]{:S(2)}, u32[]{:S(2)}) collective-permute-start(bf16[1,2,32,512]{3,2,1,0:T(8,128)(2,1)} %bitcast.368), channel_id=1, source_target_pairs={{0,16},{8,24},{16,32},{24,40},{32,48},{40,56},{48,64},{56,72},{64,... | collective-permute-start | bytes 196616 | tf_op jit(solution)/shard_map/ppermute | solution.py:17
  12.5 11.3 %collective-permute-start.1 = (bf16[1,2,32,512]{3,2,1,0:T(8,128)(2,1)}, bf16[1,2,32,512]{3,2,1,0:T(8,128)(2,1)S(1)}, u32[]{:S(2)}, u32[]{:S(2)}) collective-permute-start(bf16[1,2,32,512]{3,2,1,0:T(8,128)(2,1)} %bitcast.369), channel_id=1, source_target_pairs={{0,8},{8,16},{16,24},{24,32},{32,40},{40,48},{48,56},{56,64},{64,7... | collective-permute-start | bytes 196616 | tf_op jit(solution)/shard_map/ppermute | solution.py:17
  24.7 8.7 %copy-start.6 = (f32[16]{0:T(128)S(1)}, f32[16]{0:T(128)}, u32[]{:S(2)}) copy-start(f32[16]{0:T(128)} %param.14) | copy-start | bytes 196
  24.7 8.8 %copy-start.2 = (bf16[1,1,2,32,512]{4,3,2,1,0:T(8,128)(2,1)S(1)}, bf16[1,1,2,32,512]{4,3,2,1,0:T(8,128)(2,1)}, u32[]{:S(2)}) copy-start(bf16[1,1,2,32,512]{4,3,2,1,0:T(8,128)(2,1)} %param.12) | copy-start | bytes 196612
  24.7 2.9 collective-permute-start.2
  26.4 4.8 collective-permute-start.3
  84.1 6.6 copy-start.7
  84.1 212.0 %all-to-all-start.2 = ((bf16[32,96,3,256]{3,1,2,0:T(8,128)(2,1)}), bf16[32,96,3,256]{3,1,2,0:T(8,128)(2,1)}, u32[]{:S(2)}, u32[]{:S(2)}) async-start(bf16[32,96,3,256]{3,1,2,0:T(8,128)(2,1)} %stack.5), calls=%async_computation.2 | async-start | bytes 9437184 | tf_op jit(solution)/shard_map/all_to_all | solution.py:182
  90.4 370.6 %all-gather.3.cloned.1.call-start = ((), (), s32[]{:S(2)}) async-start(), calls=%async_computation.7 | async-start | bytes 4325376 | tf_op jit(solution)/shard_map/all_gather | solution.py:54
  110.8 205.7 %copy-start.1 = (f32[128,3072]{1,0:T(8,128)}, f32[128,3072]{1,0:T(8,128)S(1)}, u32[]{:S(2)}) copy-start(f32[128,3072]{1,0:T(8,128)S(1)} %broadcast_multiply_fusion) | copy-start | bytes 4718596
  304.4 12.1 %copy-start.5 = (f32[3072]{0:T(1024)S(1)}, f32[3072]{0:T(1024)}, u32[]{:S(2)}) copy-start(f32[3072]{0:T(1024)} %param.17) | copy-start | bytes 36868
  316.5 5.0 copy-start.4
  321.5 280.0 %all-gather.5.cloned.1.call-start = ((), (), s32[]{:S(2)}) async-start(), calls=%async_computation.8 | async-start | bytes 4325376 | tf_op jit(solution)/shard_map/all_gather | solution.py:54
  633.1 17.9 %all-to-all-start.3 = ((bf16[8,128,384]{2,1,0:T(8,128)(2,1)}), bf16[8,128,384]{2,1,0:T(8,128)(2,1)S(1)}, u32[]{:S(2)}, u32[]{:S(2)}) async-start(bf16[8,128,384]{2,1,0:T(8,128)(2,1)} %bitcast.295), calls=%async_computation.3 | async-start | bytes 1572864 | tf_op jit(solution)/shard_map/all_to_all | solution.py:65
  687.3 20.2 %all-to-all-start.6 = ((f32[64,1,384]{2,1,0:T(1,128)}), f32[64,1,384]{2,1,0:T(1,128)S(1)}, u32[]{:S(2)}, u32[]{:S(2)}) async-start(f32[64,1,384]{2,1,0:T(1,128)} %broadcast_in_dim.63), calls=%async_computation.6 | async-start | bytes 196608 | tf_op jit(solution)/shard_map/all_to_all | solution.py:35
Sparse Core Ops, SparseCore 0:
  321.6 139.3 all-gather.2
  463.0 138.4 all-gather.4
